TPU v7x, 32 devices: a whole 2x2x4 slice. The times are simulated.
32 devices in a mesh: tm: 8 (over y, x, core), input: 4 (over z).
Axes of the slice: x: 2, y: 2, z: 4, core: 2. Of those that a mesh axis runs over, the one named last changes fastest.
Arguments:
- samples: int32 [1024, 131072], P('input', 'tm'), may hold values from -16 to 16, as said below
- coefficients: float32 [8, 512], replicated, may hold values from -2 to 2
Outputs:
- visibility: bfloat16 [256, 2, 1024, 1024], P(('tm', 'input'))
Inputs may be any that keep to these rules, and one draw needn't show every extreme that they name: `samples`: noise-dominated integer voltages: each input carries independent integer noise plus a weak common signal.
All inputs are finite; a program needn't handle non-finite values.
Results may differ from a plain program's by a relative error of at most 0.007.
Values may be sent and summed in bfloat16 or wider, within the bound.
A program may use at most 192 MiB of HBM per device.

v0:
```python
import math

import jax
import jax.numpy as jnp
from jax import lax
from jax.sharding import PartitionSpec as P


def from_behind(block, axis, distance):
    devices = range(lax.axis_size(axis))
    route = [(i - distance, i) for i in devices if i - distance in devices]
    return lax.ppermute(block, axis, route)


def dft_table(length):
    row_index = jnp.arange(length, dtype=jnp.int32)
    channel = row_index // 2
    parity = row_index % 2
    positions = jnp.arange(length, dtype=jnp.int32)
    phase_index = channel[:, None] * positions[None, :] % length
    angles = phase_index.astype(jnp.float32) * (2.0 * math.pi / length)
    values = jnp.where(parity[:, None] == 0, jnp.cos(angles), -jnp.sin(angles)) / math.sqrt(length)
    return values.astype(jnp.bfloat16)


def local(samples, coefficients):
    inputs_dev, sample_count = samples.shape
    tap_count, fft_length = coefficients.shape
    frames_dev = sample_count // fft_length
    tm_count = lax.axis_size("tm")
    input_count = lax.axis_size("input")
    devices = tm_count * input_count
    frames_all = frames_dev * tm_count
    signal = (samples.astype(jnp.float32) / 8.0).reshape(inputs_dev, frames_dev, fft_length)
    tail_frames = signal[:, frames_dev - (tap_count - 1) :, :].astype(jnp.bfloat16)
    previous = from_behind(tail_frames, "tm", 1)
    extended = jnp.concatenate([previous.astype(jnp.float32), signal], axis=1)
    filtered = jnp.zeros((inputs_dev, frames_dev, fft_length), jnp.float32)
    for tap_index in range(tap_count):
        start_frame = tap_count - 1 - tap_index
        filtered = (
            filtered
            + coefficients[tap_index][None, None, :]
            * extended[:, start_frame : start_frame + frames_dev, :]
        )
    filtered = filtered.astype(jnp.bfloat16)
    spectra = jnp.einsum(
        "mn,ifn->mfi", dft_table(fft_length), filtered, preferred_element_type=jnp.float32
    ).astype(jnp.bfloat16)
    channels = fft_length // 2
    per_device = channels // devices
    outgoing = spectra.reshape(1, devices, per_device, 2 * frames_dev, inputs_dev)
    received = lax.all_to_all(outgoing, ("tm", "input"), split_axis=1, concat_axis=0, tiled=True)
    item_count = received.shape[-3]
    spectra_block = received.reshape(tm_count, input_count, item_count, 2, frames_dev, inputs_dev)
    real_part = jnp.einsum(
        "tacrfi,tbcrfj->caibj", spectra_block, spectra_block, preferred_element_type=jnp.float32
    )
    cross_part = jnp.einsum(
        "tacfi,tbcfj->caibj",
        spectra_block[:, :, :, 1],
        spectra_block[:, :, :, 0],
        preferred_element_type=jnp.float32,
    )
    imag_part = cross_part - jnp.transpose(cross_part, (0, 3, 4, 1, 2))
    full_width = input_count * inputs_dev
    stacked = jnp.stack([real_part, imag_part], axis=1).reshape(
        item_count, 2, full_width, full_width
    )
    return (stacked / frames_all).astype(jnp.bfloat16)


def solution(mesh):
    in_specs = (P("input", "tm"), P())
    out_specs = P(("tm", "input"), None, None, None)
    return jax.shard_map(local, mesh=mesh, in_specs=in_specs, out_specs=out_specs, check_vma=False)
```

profile of v0, /device:TPU:1, one launch (start us, length us, event | category | flops | bytes accessed | tf_op | source)
XLA Modules:
  0.0 628.6 jit_solution(8023938041897424621)
XLA Ops:
  0.0 6.6 %convert_multiply_fusion = f32[256,16384]{1,0:T(8,128)S(1)} fusion(s32[256,16384]{1,0:T(8,128)} %param.2), kind=kLoop, calls=%fused_computation.38 | loop fusion | flops 8388608 | bytes 33554432 | tf_op jit(solution)/shard_map/div | solution.py:34
  6.6 0.0 copy-start.2
  6.6 1.7 copy.50
  8.3 6.2 copy-done
  14.5 0.2 slice.199
  14.7 4.5 collective-permute-start
  19.3 20.1 %collective-permute-done = bf16[256,7,512]{2,0,1:T(8,128)(2,1)S(1)} collective-permute-done((bf16[256,7,512]{2,0,1:T(8,128)(2,1)S(1)}, bf16[256,7,512]{2,0,1:T(8,128)(2,1)S(1)}, u32[]{:S(2)}, u32[]{:S(2)}) %collective-permute-start) | collective-permute-done | bytes 1835040 | tf_op jit(solution)/shard_map/ppermute | solution.py:12
  39.4 0.5 convert_element_type.26
  39.9 42.8 %fusion.63 = bf16[256,32,512]{2,0,1:T(8,128)(2,1)S(1)} fusion(f32[256,32,512]{2,0,1:T(8,128)} %bitcast.49, f32[256,7,512]{2,0,1:T(8,128)S(1)} %convert_element_type.26, f32[512]{0:T(512)S(1)} %bitcast.60, f32[512]{0:T(512)S(1)} %bitcast.61, f32[512]{0:T(512)S(1)} %bitcast.55, f32[512]{0:T(512)S(1)} %bitcast.56, f32[512]{0:T(512)S(1)} %bitcast.57, ...), kind=kLoop, calls=%fused_computation.19.clone.clone.clone.clone.2 | loop fusion | flops 96468992 | bytes 28852224 | tf_op jit(solution)/shard_map/mn,ifn->mfi/dot_general | solution.py:47
  82.7 15.2 %convert_bitcast_fusion = bf16[512,32,256]{0,2,1:T(8,128)(2,1)} fusion(s32[512]{0:T(512)S(1)} %add_select_fusion.1, pred[512]{0:T(512)(128)(4,1)S(1)} %fusion.43, bf16[256,32,512]{2,0,1:T(8,128)(2,1)S(1)} %fusion.63), kind=kOutput, calls=%fused_computation.43 | convolution fusion | flops 4303880192 | bytes 16779776 | tf_op jit(solution)/shard_map/mn,ifn->mfi/dot_general | solution.py:47
  97.9 14.6 %copy.22 = bf16[512,32,256]{2,1,0:T(8,128)(2,1)} copy(bf16[512,32,256]{0,2,1:T(8,128)(2,1)} %convert_bitcast_fusion) | data formatting | bytes 16777216 | tf_op jit(solution)/shard_map/convert_element_type | solution.py:49
  112.5 190.6 %all_to_all.4 = bf16[1,32,8,64,256]{4,3,2,0,1:T(8,128)(2,1)S(1)} all-to-all(bf16[1,32,8,64,256]{4,3,2,0,1:T(8,128)(2,1)} %bitcast.53), channel_id=1, replica_groups=mesh['tm'=8,'input'=4] {'tm','input'}, dimensions={1} | all-to-all | bytes 16777216 | tf_op jit(solution)/shard_map/all_to_all | solution.py:53
  303.1 3.2 copy-done.1
  306.3 3.7 fusion.55
  310.0 19.7 %convolution_bitcast_fusion = f32[8,4,256,4,256]{4,2,3,1,0:T(8,128)} fusion(bf16[8,4,8,1,32,256]{5,4,3,2,1,0:T(8,128)(2,1)} %get-tuple-element.6, bf16[8,4,8,1,32,256]{5,4,3,2,1,0:T(8,128)(2,1)} %get-tuple-element.5), kind=kOutput, calls=%fused_computation.39 | convolution fusion | flops 4294967296 | bytes 41943040 | tf_op jit(solution)/shard_map/tacfi,tbcfj->caibj/dot_general | solution.py:59
  329.7 33.8 %copy.27 = f32[8,4,256,4,256]{2,4,1,3,0:T(8,128)} copy(f32[8,4,256,4,256]{4,2,3,1,0:T(8,128)} %convolution_bitcast_fusion) | data formatting | bytes 67108864 | tf_op jit(solution)/shard_map/tacfi,tbcfj->caibj/dot_general | solution.py:59
  363.5 33.5 %bitcast_subtract_fusion = f32[8,4,256,4,256]{4,2,3,1,0:T(8,128)} fusion(f32[8,4,256,4,256]{4,2,3,1,0:T(8,128)} %convolution_bitcast_fusion, f32[8,4,256,4,256]{2,4,1,3,0:T(8,128)} %copy.27), kind=kLoop, calls=%fused_computation.8 | loop fusion | flops 8388608 | bytes 100663296 | tf_op jit(solution)/shard_map/sub | solution.py:65
  397.1 37.9 %copy.28 = f32[8,4,256,4,256]{4,3,2,1,0:T(4,128)} copy(f32[8,4,256,4,256]{4,2,3,1,0:T(8,128)} %bitcast_subtract_fusion) | data formatting | bytes 67108864 | tf_op jit(solution)/shard_map/sub | solution.py:65
  434.9 40.5 %stack.10 = f32[8,1,1024,1024]{3,2,0,1:T(8,128)} reshape(f32[8,4,256,4,256]{4,3,2,1,0:T(4,128)} %copy.28) | data formatting | bytes 67108864 | tf_op jit(solution)/shard_map/stack | solution.py:67
  475.4 18.7 %convolution_bitcast_fusion.1 = f32[8,4,256,4,256]{4,2,3,1,0:T(8,128)} fusion(bf16[8,4,8,2,32,256,1]{5,4,3,2,1,0,6:T(8,128)(2,1)} %bitcast.52), kind=kOutput, calls=%fused_computation.40 | convolution fusion | flops 8589934592 | bytes 41943040 | tf_op jit(solution)/shard_map/tacrfi,tbcrfj->caibj/dot_general | solution.py:56
  494.1 37.9 %copy.24 = f32[8,4,256,4,256]{4,3,2,1,0:T(4,128)} copy(f32[8,4,256,4,256]{4,2,3,1,0:T(8,128)} %convolution_bitcast_fusion.1) | data formatting | bytes 67108864 | tf_op jit(solution)/shard_map/tacrfi,tbcrfj->caibj/dot_general | solution.py:56
  532.0 40.5 %stack.9 = f32[8,1,1024,1024]{3,2,0,1:T(8,128)} reshape(f32[8,4,256,4,256]{4,3,2,1,0:T(4,128)} %copy.24) | data formatting | bytes 67108864 | tf_op jit(solution)/shard_map/stack | solution.py:67
  572.5 32.9 %fusion = bf16[8,2,1024,1024]{3,2,0,1:T(8,128)(2,1)} fusion(f32[8,1,1024,1024]{3,2,0,1:T(8,128)} %stack.10, f32[8,1,1024,1024]{3,2,0,1:T(8,128)} %stack.9), kind=kLoop, calls=%fused_computation.1 | loop fusion | flops 50331648 | bytes 100663296 | tf_op jit(solution)/shard_map/convert_element_type | solution.py:70
  605.3 23.2 %copy.29 = bf16[8,2,1024,1024]{3,2,1,0:T(8,128)(2,1)} copy(bf16[8,2,1024,1024]{3,2,0,1:T(8,128)(2,1)} %fusion) | data formatting | bytes 67108864 | tf_op jit(solution)/shard_map/convert_element_type | solution.py:70
  (6 shorter events, 0.0 us)
Async XLA Ops:
  6.6 12.7 %copy-start.2 = (f32[8,512]{1,0:T(8,128)S(1)}, f32[8,512]{1,0:T(8,128)}, u32[]{:S(2)}) copy-start(f32[8,512]{1,0:T(8,128)} %param.3) | copy-start | bytes 49156
  8.3 6.2 copy-start
  14.7 24.7 %collective-permute-start = (bf16[256,7,512]{2,0,1:T(8,128)(2,1)S(1)}, bf16[256,7,512]{2,0,1:T(8,128)(2,1)S(1)}, u32[]{:S(2)}, u32[]{:S(2)}) collective-permute-start(bf16[256,7,512]{2,0,1:T(8,128)(2,1)S(1)} %slice.199), channel_id=1, source_target_pairs={{0,4},{4,8},{8,12},{12,16},{16,20},{20,24},{24,28},{1,5},{5,9},{9,... | collective-permute-start | bytes 5505032 | tf_op jit(solution)/shard_map/ppermute | solution.py:12
  303.1 3.2 copy-start.1
where the time goes:
time: 631 us; the launch traced here: 629 us
  local copies, waits for them, and re-layouts  243 us (39%)
  blocking collectives  191 us (30%)
  other arithmetic  116 us (18%)
  matrix products  53.6 us (8%)
  waiting for transfers between devices  20.1 us (3%)
    all_to_all x1, blocking collectives, local(): lax.all_to_all(outgoing, ('tm', 'input'), split_axis=1, concat_axis=0, ti...  191 us
    another operation x2, local copies, waits for them, and re-layouts, local(): jnp.stack([real_part, imag_part], axis=1)  80.9 us
    dot_general x1, other arithmetic, local(): jnp.einsum('mn,ifn->mfi', dft_table(fft_length), filtered, preferred_elem...  42.8 us
    dot_general x1, local copies, waits for them, and re-layouts, local(): jnp.einsum('tacrfi,tbcrfj->caibj', spectra_block, spectra_block, preferre...  37.9 us
    sub x1, local copies, waits for them, and re-layouts, local(): imag_part = cross_part - jnp.transpose(cross_part, (0, 3, 4, 1, 2))  37.9 us
    dot_general x1, local copies, waits for them, and re-layouts, local(): jnp.einsum('tacfi,tbcfj->caibj', spectra_block[:, :, :, 1], spectra_block...  33.8 us
    sub x1, other arithmetic, local(): imag_part = cross_part - jnp.transpose(cross_part, (0, 3, 4, 1, 2))  33.5 us
    convert_element_type x1, other arithmetic, local(): return (stacked / frames_all).astype(jnp.bfloat16)  32.9 us
  transfers between devices with their start and end apart: 1, of which 1 were waited for; matrix products, arithmetic and copies ran while one was open for 0% of the time, Pallas kernels for 0%

commit v1 on v0

v1 whole, which is shorter than its diff:
```python
import functools
import math

import jax
import jax.numpy as jnp
import ml_dtypes
import numpy as np
from jax import lax
from jax.experimental import pallas as pl
from jax.experimental.pallas import tpu as pltpu
from jax.sharding import PartitionSpec as P

MESH = pl.DeviceIdType.MESH
GROUP = 16
UNIT = 8


def dft_table(length):
    row = np.arange(length)
    phase = ((row // 2)[:, None] * np.arange(length)[None, :]) % length
    angles = phase.astype(np.float32) * np.float32(2.0 * math.pi / length)
    values = np.where((row % 2)[:, None] == 0, np.cos(angles), -np.sin(angles))
    return (values / np.float32(math.sqrt(length))).astype(ml_dtypes.bfloat16)


def reorder_matrix():
    size = GROUP * GROUP
    target = np.arange(size)
    matrix = np.zeros((size, size), np.float32)
    matrix[target, (target % GROUP) * GROUP + target // GROUP] = 1.0
    return matrix.astype(ml_dtypes.bfloat16)


def partner(me, step, count):
    if count & (count - 1):
        return lax.rem(me + step, count)
    result = 0
    bit = 1
    while bit < count:
        flipped = lax.rem(lax.div(me, bit) + lax.div(step, bit), 2)
        result = result + bit * flipped
        bit *= 2
    return result


def exchange_kernel(
    tm_count,
    input_count,
    samples_ref,
    coef_ref,
    table_ref,
    reorder_ref,
    recv_ref,
    stage,
    signal,
    halo_out,
    halo_in,
    filtered,
    spectra,
    send,
    load_sem,
    halo_sem,
    send_sem,
    recv_sem,
    own_sem,
):
    devices = tm_count * input_count
    taps, length = coef_ref.shape
    inputs = samples_ref.shape[0]
    frames = samples_ref.shape[1] // length
    halo = taps - 1
    units = frames // UNIT
    groups = frames // GROUP
    rows = length // devices
    tm = lax.axis_index("tm")
    me = tm * input_count + lax.axis_index("input")

    def load(unit):
        return pltpu.make_async_copy(
            samples_ref.at[:, pl.ds(unit * UNIT * length, UNIT * length)],
            stage.at[unit % 2],
            load_sem.at[unit % 2],
        )

    load(units - 1).start()
    if units > 1:
        load(units - 2).start()

    def place(device):
        return {"tm": lax.div(device, input_count), "input": lax.rem(device, input_count)}

    barrier = pltpu.get_barrier_semaphore()

    def greet(step, carry):
        pl.semaphore_signal(
            barrier, inc=1, device_id=place(partner(me, step, devices)), device_id_type=MESH
        )
        return carry

    lax.fori_loop(1, devices, greet, 0)

    def convert(unit):
        load(unit).wait()
        for frame in range(UNIT):

            def chunk(k, carry):
                at = pl.ds(pl.multiple_of(k * 32, 32), 32)
                values = stage[unit % 2, at, frame * length : (frame + 1) * length]
                values = values.astype(jnp.float32) * 0.125
                signal[halo + unit * UNIT + frame, at, :] = values
                if unit == units - 1 and frame >= UNIT - halo:
                    halo_out[frame - (UNIT - halo), at, :] = values.astype(jnp.bfloat16)
                return carry

            lax.fori_loop(0, inputs // 32, chunk, 0)
        if unit >= 2:
            load(unit - 2).start()

    convert(units - 1)
    pl.semaphore_wait(barrier, devices - 1)
    halo_copy = pltpu.make_async_remote_copy(
        src_ref=halo_out,
        dst_ref=halo_in,
        send_sem=halo_sem.at[0],
        recv_sem=halo_sem.at[1],
        device_id={"tm": lax.rem(tm + 1, tm_count), "input": lax.axis_index("input")},
        device_id_type=MESH,
    )
    halo_copy.start()

    next_unit = units - 2
    for group in reversed(range(groups)):
        first = group * GROUP
        while next_unit >= 0 and (next_unit + 1) * UNIT > first - halo:
            convert(next_unit)
            next_unit -= 1
        if group == 0:
            halo_copy.wait()
            keep = jnp.where(tm == 0, 0.0, 1.0)

            def unpack(index, carry):
                at = pl.ds(pl.multiple_of(lax.rem(index, inputs // 32) * 32, 32), 32)
                frame = lax.div(index, inputs // 32)
                signal[frame, at, :] = halo_in[frame, at, :].astype(jnp.float32) * keep
                return carry

            lax.fori_loop(0, halo * (inputs // 32), unpack, 0)

        def one_frame(frame, carry):
            def chunk(k, inner):
                at = pl.ds(pl.multiple_of(k * 32, 32), 32)
                total = coef_ref[0:1, :] * signal[first + frame + halo, at, :]
                for tap in range(1, taps):
                    total = total + coef_ref[tap : tap + 1, :] * signal[
                        first + frame + halo - tap, at, :
                    ]
                filtered[at, :] = total.astype(jnp.bfloat16)
                return inner

            lax.fori_loop(0, inputs // 32, chunk, 0)
            spectra[frame] = lax.dot_general(
                table_ref[...],
                filtered[...],
                (((1,), (1,)), ((), ())),
                preferred_element_type=jnp.float32,
            ).astype(jnp.bfloat16)
            return carry

        lax.fori_loop(0, GROUP, one_frame, 0)

        def reorder(block):
            at = pl.multiple_of(block * GROUP, GROUP)
            part = spectra[:, pl.ds(at, GROUP), :].reshape(GROUP * GROUP, inputs)
            part = jnp.dot(reorder_ref[...], part, preferred_element_type=jnp.float32)
            part = part.astype(jnp.bfloat16).reshape(GROUP, GROUP, inputs)
            send[group, pl.ds(at, GROUP)] = part

        blocks = rows // GROUP
        if blocks * GROUP != rows:

            def reorder_one(block, carry):
                reorder(block)
                return carry

            lax.fori_loop(0, length // GROUP, reorder_one, 0)

        def send_one(step, carry):
            target = partner(me, step, devices)
            if blocks * GROUP == rows:
                for block in range(blocks):
                    reorder(target * blocks + block)
            pltpu.make_async_remote_copy(
                src_ref=send.at[group, pl.ds(target * rows, rows)],
                dst_ref=recv_ref.at[group, me],
                send_sem=send_sem.at[group],
                recv_sem=recv_sem.at[group],
                device_id=place(target),
                device_id_type=MESH,
            ).start()
            return carry

        lax.fori_loop(1, devices, send_one, 0)
        if blocks * GROUP == rows:
            for block in range(blocks):
                reorder(me * blocks + block)
        pltpu.make_async_copy(
            send.at[group, pl.ds(me * rows, rows)], recv_ref.at[group, me], own_sem.at[group]
        ).start()

    for group in reversed(range(groups)):
        pltpu.make_async_copy(
            send.at[group, pl.ds(me * rows, rows)], recv_ref.at[group, me], own_sem.at[group]
        ).wait()
        sent = send.at[group, pl.ds(0, (devices - 1) * rows)]
        pltpu.make_async_copy(sent, sent, send_sem.at[group]).wait()
        got = recv_ref.at[group, pl.ds(0, devices - 1)]
        pltpu.make_async_copy(got, got, recv_sem.at[group]).wait()


def correlate_kernel(frames_all, recv_ref, out_ref, left, right):
    groups, tm_count, input_count, _, _, _, inputs = recv_ref.shape
    depth = groups * tm_count * GROUP
    width = input_count * inputs
    for z in range(input_count):
        at = slice(z * inputs, (z + 1) * inputs)
        past = slice(width + z * inputs, width + (z + 1) * inputs)
        real = recv_ref[:, :, z, 0, 0].reshape(depth, inputs)
        imag = recv_ref[:, :, z, 0, 1].reshape(depth, inputs)
        right[:depth, at] = real
        right[depth:, at] = imag
        right[:depth, past] = -imag
        right[depth:, past] = real
        left[at, :depth] = real.T
        left[at, depth:] = imag.T
    tile = 256
    columns = 512

    def one_row(k, carry):
        at = pl.ds(pl.multiple_of(k * tile, tile), tile)
        for part in range(2):
            for column in range(0, width, columns):
                start = part * width + column
                total = jnp.dot(
                    left[at, :],
                    right[:, start : start + columns],
                    preferred_element_type=jnp.float32,
                )
                out_ref[0, part, at, column : column + columns] = (
                    total * (1.0 / frames_all)
                ).astype(jnp.bfloat16)
        return carry

    lax.fori_loop(0, width // tile, one_row, 0)


def local(samples, coefficients):
    inputs, sample_count = samples.shape
    taps, length = coefficients.shape
    frames = sample_count // length
    tm_count = lax.axis_size("tm")
    input_count = lax.axis_size("input")
    devices = tm_count * input_count
    groups = frames // GROUP
    rows = length // devices
    per_device = rows // 2
    bf16 = jnp.bfloat16
    vmem = pl.BlockSpec(memory_space=pltpu.VMEM)
    anywhere = pl.BlockSpec(memory_space=pl.ANY)
    received = pl.pallas_call(
        functools.partial(exchange_kernel, tm_count, input_count),
        out_shape=jax.ShapeDtypeStruct((groups, devices, rows, GROUP, inputs), bf16),
        in_specs=[anywhere, vmem, vmem, vmem],
        out_specs=anywhere,
        scratch_shapes=[
            pltpu.VMEM((2, inputs, UNIT * length), jnp.int32),
            pltpu.VMEM((frames + taps - 1, inputs, length), jnp.float32),
            pltpu.VMEM((taps - 1, inputs, length), bf16),
            pltpu.VMEM((taps - 1, inputs, length), bf16),
            pltpu.VMEM((inputs, length), bf16),
            pltpu.VMEM((GROUP, length, inputs), bf16),
            pltpu.VMEM((groups, length, GROUP, inputs), bf16),
            pltpu.SemaphoreType.DMA((2,)),
            pltpu.SemaphoreType.DMA((2,)),
            pltpu.SemaphoreType.DMA((groups,)),
            pltpu.SemaphoreType.DMA((groups,)),
            pltpu.SemaphoreType.DMA((groups,)),
        ],
        compiler_params=pltpu.CompilerParams(
            collective_id=0, has_side_effects=True, vmem_limit_bytes=56 * 2**20
        ),
        name="channelise_exchange",
    )(samples, coefficients, jnp.asarray(dft_table(length)), jnp.asarray(reorder_matrix()))
    received = received.reshape(groups, tm_count, input_count, per_device, 2, GROUP, inputs)
    width = input_count * inputs
    depth = frames * tm_count
    return pl.pallas_call(
        functools.partial(correlate_kernel, depth),
        grid=(per_device,),
        out_shape=jax.ShapeDtypeStruct((per_device, 2, width, width), bf16),
        in_specs=[
            pl.BlockSpec(
                (groups, tm_count, input_count, 1, 2, GROUP, inputs),
                lambda c: (0, 0, 0, c, 0, 0, 0),
            )
        ],
        out_specs=pl.BlockSpec((1, 2, width, width), lambda c: (c, 0, 0, 0)),
        scratch_shapes=[
            pltpu.VMEM((width, 2 * depth), bf16),
            pltpu.VMEM((2 * depth, 2 * width), bf16),
        ],
        compiler_params=pltpu.CompilerParams(vmem_limit_bytes=48 * 2**20),
        name="correlate",
    )(received)


def solution(mesh):
    in_specs = (P("input", "tm"), P())
    out_specs = P(("tm", "input"), None, None, None)
    return jax.shard_map(local, mesh=mesh, in_specs=in_specs, out_specs=out_specs, check_vma=False)
```

time: 631 us -> 236 us (0.37)
  local copies, waits for them, and re-layouts: 243 us -> 0 us
  Pallas kernels: 0 us -> 235 us
  blocking collectives: 191 us -> 0 us
  other arithmetic: 116 us -> 0 us
  matrix products: 53.6 us -> 0 us
  waiting for transfers between devices: 20.1 us -> 0 us
    pallas_call x0 -> x2, Pallas kernels: none -> 235 us  [the longest x1 205 us: local(): pl.pallas_call(functools.partial(exchange_kernel, tm_count, input_count),...]
    all_to_all x1 -> x0, blocking collectives: 191 us -> none  [local(): lax.all_to_all(outgoing, ('tm', 'input'), split_axis=1, concat_axis=0, ti...]
    another operation x2 -> x0, local copies, waits for them, and re-layouts: 80.9 us -> none  [local(): jnp.stack([real_part, imag_part], axis=1)]
    dot_general x2 -> x0, local copies, waits for them, and re-layouts: 71.7 us -> none  [the longest x1 37.9 us: local(): jnp.einsum('tacrfi,tbcrfj->caibj', spectra_block, spectra_block, preferre...]
    dot_general x3 -> x0, matrix products: 53.6 us -> none  [the longest x1 19.7 us: local(): jnp.einsum('tacfi,tbcfj->caibj', spectra_block[:, :, :, 1], spectra_block...]
    dot_general x1 -> x0, other arithmetic: 42.8 us -> none  [local(): jnp.einsum('mn,ifn->mfi', dft_table(fft_length), filtered, preferred_elem...]
    convert_element_type x2 -> x0, local copies, waits for them, and re-layouts: 37.9 us -> none  [the longest x1 23.2 us: local(): return (stacked / frames_all).astype(jnp.bfloat16)]
    sub x1 -> x0, local copies, waits for them, and re-layouts: 37.9 us -> none  [local(): imag_part = cross_part - jnp.transpose(cross_part, (0, 3, 4, 1, 2))]
  transfers between devices with their start and end apart: 1 -> 0, of which waited for: 1 -> 0; matrix products, arithmetic and copies ran while one was open for 0% -> 0% of each run, Pallas kernels for 0% -> 0%
where the time goes in v1:
time: 236 us; the launch traced here: 235 us
  Pallas kernels  235 us (100%)
    pallas_call x1, Pallas kernels, local(): pl.pallas_call(functools.partial(exchange_kernel, tm_count, input_count),...  205 us
    pallas_call x1, Pallas kernels, local(): pl.pallas_call(functools.partial(correlate_kernel, depth), grid=(per_devi...  29.9 us

profile of v1, /device:TPU:1, one launch (start us, length us, event | category | flops | bytes accessed | tf_op | source)
XLA Modules:
  0.0 235.3 jit_solution(3181580119401991549)
XLA Ops:
  0.0 205.4 %channelise_exchange.1 = bf16[2,32,16,16,256]{4,3,2,1,0:T(8,128)(2,1)} custom-call(s32[256,16384]{1,0:T(8,128)} %samples_ref.1, f32[8,512]{1,0:T(8,128)} %coef_ref.1, bf16[512,512]{1,0:T(8,128)(2,1)} %constant.4.clone.table_ref, bf16[256,256]{1,0:T(8,128)(2,1)} %constant.5.clone.reorder_ref), custom_call_target="tpu_custom_call" | custom-call | tf_op jit(solution)/shard_map/channelise_exchange/pallas_call | solution.py:269
  205.4 29.9 %correlate.1 = bf16[8,2,1024,1024]{3,2,1,0:T(8,128)(2,1)} custom-call(bf16[2,8,4,8,2,16,256]{6,5,4,3,2,1,0:T(8,128)(2,1)} %bitcast.1), custom_call_target="tpu_custom_call" | custom-call | tf_op jit(solution)/shard_map/correlate/pallas_call | solution.py:296
